TPU v7x, 32 devices: a whole 2x2x4 slice. The times are simulated.
32 devices in a mesh: dp: 8 (over z, y), tensor: 4 (over x, core).
Axes of the slice: x: 2, y: 2, z: 4, core: 2. Of those that a mesh axis runs over, the one named last changes fastest.
Arguments:
- inputs: bfloat16 [25600, 768], P(('dp', 'tensor')), may hold values from -6 to 6
- res_ids: int32 [32], P(('dp', 'tensor')), may hold values from 0 to 1
- memory: bfloat16 [2, 6400, 768], P(None, ('dp', 'tensor')), may hold values from -6 to 6
- gain_one: float32 [768], replicated, may hold values from 0.5 to 1.5
- bias_one: float32 [768], replicated, may hold values from -1.8 to 1.8
- w_qkv: bfloat16 [768, 2304], replicated, may hold values from -0.21875 to 0.21875
- b_qkv: float32 [2304], replicated, may hold values from -1.8 to 1.8
- pool_weight: float32 [3, 27, 96], replicated, may hold values from -1.25 to 1.25
- pool_gain: float32 [3, 96], replicated, may hold values from 0.5 to 1.5
- pool_bias: float32 [3, 96], replicated, may hold values from -1.8 to 1.8
- rel_table: float32 [53, 96], replicated, may hold values from -0.6 to 0.6
- w_proj: bfloat16 [768, 768], replicated, may hold values from -0.21875 to 0.21875
- b_proj: float32 [768], replicated, may hold values from -1.8 to 1.8
- gain_two: float32 [768], replicated, may hold values from 0.5 to 1.5
- bias_two: float32 [768], replicated, may hold values from -1.8 to 1.8
- w_up: bfloat16 [768, 3072], P(None, 'tensor'), may hold values from -0.21875 to 0.21875
- b_up: bfloat16 [3072], P('tensor'), may hold values from -1.796875 to 1.796875
- w_down: bfloat16 [3072, 768], P('tensor'), may hold values from -0.109375 to 0.109375
- b_down: float32 [768], replicated, may hold values from -1.8 to 1.8
- cotangent: bfloat16 [25600, 768], P(('dp', 'tensor')), may hold values from -6 to 6
Outputs:
- output: bfloat16 [25600, 768], P(('dp', 'tensor'))
- input_grad: float32 [25600, 768], P(('dp', 'tensor'))
- grad_gain_one: float32 [768], replicated
- grad_bias_one: float32 [768], replicated
- grad_w_qkv: float32 [768, 2304], replicated
- grad_b_qkv: float32 [2304], replicated
- grad_pool_weight: float32 [3, 27, 96], replicated
- grad_pool_gain: float32 [3, 96], replicated
- grad_pool_bias: float32 [3, 96], replicated
- grad_rel_table: float32 [53, 96], replicated
- grad_w_proj: float32 [768, 768], replicated
- grad_b_proj: float32 [768], replicated
- grad_gain_two: float32 [768], replicated
- grad_bias_two: float32 [768], replicated
- grad_w_up: float32 [768, 3072], P(None, 'tensor')
- grad_b_up: float32 [3072], P('tensor')
- grad_w_down: float32 [3072, 768], P('tensor')
- grad_b_down: float32 [768], replicated
Inputs may be any that keep to these rules, and one draw needn't show every extreme that they name: `res_ids`: 0 marks a clip whose frames hold 7 x 7 tokens in the corner of the 10 x 10 grid, 1 a clip that fills it.
All inputs are finite; a program needn't handle non-finite values.
Results may differ from a plain program's by a relative error of at most 0.012.
Values may be sent and summed in bfloat16 or wider, within the bound.
A program may use at most 384 MiB of HBM per device.

v0:
```python
import jax
import jax.numpy as jnp
from jax import lax
from jax.sharding import PartitionSpec as P

D = 768
HEADS = 8
HEAD_DIM = 96
FRAMES = 8
SIDE = 10
SMALL_SIDE = 7
LENGTH = 800
MEM = 200
OFFSETS = 28
REL_ROWS = 53
HIGHEST = lax.Precision.HIGHEST
NORM_EPS = 1e-06
INV_ROOT_TWO = 0.7071067811865476


def layer_norm(values, gain_vec, shift_vec):
    average = jnp.mean(values, axis=-1, keepdims=True)
    centered = values - average
    variance = jnp.mean(centered * centered, axis=-1, keepdims=True)
    return centered * lax.rsqrt(variance + NORM_EPS) * gain_vec + shift_vec


def gelu_exact(values):
    return 0.5 * values * (1.0 + lax.erf(values * INV_ROOT_TWO))


def grid_tables(res_ids):
    position = jnp.arange(LENGTH, dtype=jnp.int32)
    frame_of = position // (SIDE * SIDE)
    row_of = position // SIDE % SIDE
    column_of = position % SIDE
    large_clip = res_ids[:, None] == 1
    inside = (row_of < SMALL_SIDE) & (column_of < SMALL_SIDE)
    token_valid = large_clip | inside[None, :]
    memory_side = (SIDE + 1) // 2
    memory_small = (SMALL_SIDE + 1) // 2
    memory_index = jnp.arange(MEM, dtype=jnp.int32) % (MEM // 2)
    memory_row = memory_index // memory_side % memory_side
    memory_column = memory_index % memory_side
    memory_inside = (memory_row < memory_small) & (memory_column < memory_small)
    memory_valid = large_clip | memory_inside[None, :]
    frame_range = jnp.arange(FRAMES, dtype=jnp.int32)
    side_range = jnp.arange(SIDE, dtype=jnp.int32)
    row_base = 2 * FRAMES - 1
    column_base = row_base + 2 * SIDE - 1
    target = jnp.concatenate(
        [
            frame_of[:, None] - frame_range[None, :] + FRAMES - 1,
            row_base + row_of[:, None] - side_range[None, :] + SIDE - 1,
            column_base + column_of[:, None] - side_range[None, :] + SIDE - 1,
        ],
        axis=1,
    )
    select_table = (
        target[:, :, None] == jnp.arange(REL_ROWS, dtype=jnp.int32)[None, None, :]
    ).astype(jnp.float32)
    key_onehot = jnp.concatenate(
        [
            frame_of[:, None] == frame_range[None, :],
            row_of[:, None] == side_range[None, :],
            column_of[:, None] == side_range[None, :],
        ],
        axis=1,
    ).astype(jnp.float32)
    return (token_valid, memory_valid, select_table, key_onehot)


def pool_field(field, kernel):
    kernel_wide = jnp.tile(kernel, (1, HEADS))
    padded = jnp.pad(field, ((0, 0), (1, 1), (1, 1), (1, 1), (0, 0)))
    accumulated = jnp.zeros_like(field)
    for kernel_tap in range(27):
        frame_shift = kernel_tap // 9
        row_shift = kernel_tap // 3 % 3
        column_shift = kernel_tap % 3
        window = padded[
            :,
            frame_shift : frame_shift + FRAMES,
            row_shift : row_shift + SIDE,
            column_shift : column_shift + SIDE,
            :,
        ]
        accumulated = accumulated + window * kernel_wide[kernel_tap]
    return accumulated


def pool_norm(stacked, pool_weight, pool_gain, pool_bias):
    clip_count = stacked.shape[1]
    results = []
    for branch_index in range(3):
        pooled = pool_field(stacked[branch_index], pool_weight[branch_index])
        per_head = pooled.reshape(clip_count, LENGTH, HEADS, HEAD_DIM)
        results.append(layer_norm(per_head, pool_gain[branch_index], pool_bias[branch_index]))
    return jnp.stack(results)


def build_offsets(queries, rel_table, select_table):
    rel_scores = jnp.einsum("...lhe,re->...lhr", queries, rel_table, precision=HIGHEST)
    return jnp.einsum("...lhr,lpr->...lhp", rel_scores, select_table, precision=HIGHEST)


def extend_last(array_in, width_to):
    extra_cols = width_to - array_in.shape[-1]
    widths = [(0, 0)] * (array_in.ndim - 1) + [(0, extra_cols)]
    return jnp.pad(array_in, widths)


def per_device(
    inputs,
    res_ids,
    memory,
    gain_one,
    bias_one,
    w_qkv,
    b_qkv,
    pool_weight,
    pool_gain,
    pool_bias,
    rel_table,
    w_proj,
    b_proj,
    gain_two,
    bias_two,
    w_up,
    b_up,
    w_down,
    b_down,
    cotangent,
):
    clip_count = res_ids.shape[0]
    row_total = inputs.shape[0]
    scale_factor = HEAD_DIM ** (-0.5)
    ext_width = (HEAD_DIM + OFFSETS + 127) // 128 * 128
    token_valid, memory_valid, select_table, key_onehot = grid_tables(res_ids)
    token_weight = token_valid.reshape(-1).astype(jnp.float32)[:, None]
    wide_inputs = inputs.astype(jnp.float32)
    normed_one, norm_one_back = jax.vjp(layer_norm, wide_inputs, gain_one, bias_one)
    normed_low = normed_one.astype(jnp.bfloat16)
    qkv = jnp.dot(normed_low, w_qkv, preferred_element_type=jnp.float32) + b_qkv
    masked = qkv * token_weight
    stacked = jnp.moveaxis(masked.reshape(clip_count, FRAMES, SIDE, SIDE, 3, D), 4, 0)
    pooled, pool_back = jax.vjp(pool_norm, stacked, pool_weight, pool_gain, pool_bias)
    queries = pooled[0]
    offsets, offset_back = jax.vjp(
        lambda query_in, table_in: build_offsets(query_in, table_in, select_table),
        queries,
        rel_table,
    )
    query_ext = extend_last(
        jnp.concatenate([queries * scale_factor, offsets], axis=-1), ext_width
    ).astype(jnp.bfloat16)
    onehot_heads = jnp.broadcast_to(
        key_onehot[None, :, None, :], (clip_count, LENGTH, HEADS, OFFSETS)
    )
    keys_current = extend_last(
        jnp.concatenate(
            [pooled[1].astype(jnp.bfloat16), onehot_heads.astype(jnp.bfloat16)], axis=-1
        ),
        ext_width,
    )
    memory_heads = memory.reshape(2, clip_count, MEM, HEADS, HEAD_DIM)
    keys_memory = extend_last(memory_heads[0], ext_width)
    keys_ext = jnp.concatenate([keys_current, keys_memory], axis=1)
    values_all = jnp.concatenate([pooled[2].astype(jnp.bfloat16), memory_heads[1]], axis=1)
    valid_all = jnp.concatenate([token_valid, memory_valid], axis=1)[:, None, None, :]

    def masked_scores():
        raw_scores = jnp.einsum(
            "cqhx,ckhx->chqk", query_ext, keys_ext, preferred_element_type=jnp.float32
        )
        return jnp.where(valid_all, raw_scores, -1e30)

    scores = masked_scores()
    row_top = jnp.max(scores, axis=-1, keepdims=True)
    exponents = jnp.exp(scores - row_top)
    row_sum = jnp.sum(exponents, axis=-1, keepdims=True)
    probabilities = exponents / row_sum
    log_total = row_top + jnp.log(row_sum)
    weighted = jnp.einsum(
        "chqk,ckhe->cqhe",
        probabilities.astype(jnp.bfloat16),
        values_all,
        preferred_element_type=jnp.float32,
    )
    attended = (weighted + queries).reshape(row_total, D)
    attended_low = attended.astype(jnp.bfloat16)
    middle = (
        wide_inputs + jnp.dot(attended_low, w_proj, preferred_element_type=jnp.float32) + b_proj
    )
    normed_two, norm_two_back = jax.vjp(layer_norm, middle, gain_two, bias_two)
    rows_low = normed_two.astype(jnp.bfloat16)
    grad_out = cotangent.astype(jnp.float32) * token_weight
    grad_b_down = jnp.sum(grad_out, axis=0)
    grad_out_low = grad_out.astype(jnp.bfloat16)
    gathered = lax.all_gather(rows_low, "tensor", axis=0, tiled=True)
    hidden = jnp.dot(gathered, w_up, preferred_element_type=jnp.float32) + b_up.astype(jnp.float32)
    activated, gelu_back = jax.vjp(gelu_exact, hidden)
    act_low = activated.astype(jnp.bfloat16)
    row_piece = act_low
    mlp_sum = lax.psum_scatter(
        jnp.dot(row_piece, w_down, preferred_element_type=jnp.float32).astype(jnp.bfloat16),
        "tensor",
        scatter_dimension=0,
        tiled=True,
    ).astype(jnp.float32)
    grad_rows = lax.all_gather(grad_out_low, "tensor", axis=0, tiled=True)
    grad_w_down = jnp.einsum("rf,rd->fd", act_low, grad_rows, preferred_element_type=jnp.float32)
    grad_act = jnp.einsum("rd,fd->rf", grad_rows, w_down, preferred_element_type=jnp.float32)
    grad_hidden = gelu_back(grad_act)[0]
    grad_b_up = jnp.sum(grad_hidden, axis=0)
    hidden_low = grad_hidden.astype(jnp.bfloat16)
    grad_w_up = jnp.einsum("rd,rf->df", gathered, hidden_low, preferred_element_type=jnp.float32)
    row_piece = hidden_low
    grad_normed_two = lax.psum_scatter(
        jnp.einsum("rf,df->rd", row_piece, w_up, preferred_element_type=jnp.float32),
        "tensor",
        scatter_dimension=0,
        tiled=True,
    )
    output = ((middle + mlp_sum + b_down) * token_weight).astype(jnp.bfloat16)
    grad_from_two = norm_two_back(grad_normed_two)
    grad_middle = grad_out + grad_from_two[0]
    grad_b_proj = jnp.sum(grad_middle, axis=0)
    proj_low = grad_middle.astype(jnp.bfloat16)
    grad_w_proj = jnp.einsum(
        "rd,re->de", attended_low, proj_low, preferred_element_type=jnp.float32
    )
    grad_attended = jnp.einsum("re,de->rd", proj_low, w_proj, preferred_element_type=jnp.float32)
    grad_attended = grad_attended.reshape(clip_count, LENGTH, HEADS, HEAD_DIM)
    weighted_low = grad_attended.astype(jnp.bfloat16)
    probabilities = jnp.exp(masked_scores() - log_total)
    grad_probs = jnp.einsum(
        "cqhe,ckhe->chqk", weighted_low, values_all, preferred_element_type=jnp.float32
    )
    inner_sum = jnp.sum(probabilities * grad_probs, axis=-1, keepdims=True)
    grad_scores = (probabilities * (grad_probs - inner_sum)).astype(jnp.bfloat16)
    grad_query_ext = jnp.einsum(
        "chqk,ckhx->cqhx", grad_scores, keys_ext, preferred_element_type=jnp.float32
    )
    grad_key_ext = jnp.einsum(
        "chqk,cqhx->ckhx", grad_scores[..., :LENGTH], query_ext, preferred_element_type=jnp.float32
    )
    grad_values = jnp.einsum(
        "chqk,cqhe->ckhe",
        probabilities[..., :LENGTH].astype(jnp.bfloat16),
        weighted_low,
        preferred_element_type=jnp.float32,
    )
    offset_grads = offset_back(grad_query_ext[..., HEAD_DIM : HEAD_DIM + OFFSETS])
    grad_queries = grad_query_ext[..., :HEAD_DIM] * scale_factor + grad_attended + offset_grads[0]
    pool_grads = pool_back(jnp.stack([grad_queries, grad_key_ext[..., :HEAD_DIM], grad_values]))
    grad_qkv = jnp.moveaxis(pool_grads[0], 0, 4).reshape(row_total, 3 * D) * token_weight
    grad_b_qkv = jnp.sum(grad_qkv, axis=0)
    qkv_low = grad_qkv.astype(jnp.bfloat16)
    grad_w_qkv = jnp.einsum("rd,rq->dq", normed_low, qkv_low, preferred_element_type=jnp.float32)
    grad_normed_one = jnp.einsum("rq,dq->rd", qkv_low, w_qkv, preferred_element_type=jnp.float32)
    grad_from_one = norm_one_back(grad_normed_one)
    input_grad = grad_middle + grad_from_one[0]
    summed = lax.psum(
        (
            grad_from_one[1],
            grad_from_one[2],
            grad_w_qkv,
            grad_b_qkv,
            pool_grads[1],
            pool_grads[2],
            pool_grads[3],
            offset_grads[1],
            grad_w_proj,
            grad_b_proj,
            grad_from_two[1],
            grad_from_two[2],
            grad_b_down,
        ),
        ("dp", "tensor"),
    )
    mlp_summed = lax.psum((grad_w_up, grad_b_up, grad_w_down), "dp")
    return (
        output,
        input_grad,
        summed[0],
        summed[1],
        summed[2],
        summed[3],
        summed[4],
        summed[5],
        summed[6],
        summed[7],
        summed[8],
        summed[9],
        summed[10],
        summed[11],
        mlp_summed[0],
        mlp_summed[1],
        mlp_summed[2],
        summed[12],
    )


def solution(mesh):
    return jax.shard_map(
        per_device,
        mesh=mesh,
        in_specs=(
            P(("dp", "tensor"), None),
            P(("dp", "tensor")),
            P(None, ("dp", "tensor"), None),
            P(),
            P(),
            P(),
            P(),
            P(),
            P(),
            P(),
            P(),
            P(),
            P(),
            P(),
            P(),
            P(None, "tensor"),
            P("tensor"),
            P("tensor", None),
            P(),
            P(("dp", "tensor"), None),
        ),
        out_specs=(
            P(("dp", "tensor"), None),
            P(("dp", "tensor"), None),
            P(),
            P(),
            P(),
            P(),
            P(),
            P(),
            P(),
            P(),
            P(),
            P(),
            P(),
            P(),
            P(None, "tensor"),
            P("tensor"),
            P("tensor", None),
            P(),
        ),
        check_vma=False,
    )
```

profile of v0, /device:TPU:0, one launch (start us, length us, event | category | flops | bytes accessed | tf_op | source)
XLA Modules:
  0.0 2125.4 jit_solution(17922374645029894747)
XLA Ops:
  108.8 15.1 slice_bitcast_fusion.7
  125.5 69.1 %add_reduce_fusion.2 = f32[8,10,10,768]{3,2,1,0:T(8,128)} fusion(f32[768]{0:T(1024)S(1)} %copy-done.108, f32[768]{0:T(1024)S(1)} %copy-done.136, f32[768]{0:T(1024)S(1)} %copy-done.144, f32[768]{0:T(1024)S(1)} %copy-done.147, f32[768]{0:T(1024)S(1)} %copy-done.150, f32[768]{0:T(1024)S(1)} %copy-done.153, f32[768]{0:T(1024)S(1)} %copy-done.155, ...), kind=kLoop, calls=%fused_computation.210 | loop fusion | flops 32563200 | bytes 7455744 | tf_op jit(solution)/shard_map/jvp()/add | solution.py:88
  268.0 76.3 %add_reduce_fusion.1 = f32[8,10,10,768]{3,2,1,0:T(8,128)} fusion(f32[768]{0:T(1024)S(1)} %tile.497, f32[768]{0:T(1024)} %tile.495, f32[768]{0:T(1024)} %tile.493, f32[768]{0:T(1024)} %tile.491, f32[768]{0:T(1024)} %tile.489, f32[768]{0:T(1024)} %tile.487, f32[768]{0:T(1024)} %tile.485, f32[768]{0:T(1024)} %tile.483, f32[768]{0:T(1024)} %tile.481, ...), kind=kLoop, calls=%fused_computation.208 | loop fusion | flops 32563200 | bytes 7455744 | tf_op jit(solution)/shard_map/jvp()/add | solution.py:88
  420.0 76.1 %fusion.116 = (f32[8,10,10,768]{3,2,1,0:T(8,128)}, f32[1,8,10,10,768]{4,0,3,2,1:T(1,128)}) fusion(f32[768]{0:T(1024)} %tile.443, f32[768]{0:T(1024)} %tile.441, f32[768]{0:T(1024)} %tile.439, f32[768]{0:T(1024)} %tile.437, f32[768]{0:T(1024)} %tile.435, f32[768]{0:T(1024)} %tile.433, f32[768]{0:T(1024)} %tile.431, f32[768]{0:T(1024)} %tile.429, ...), kind=kLoop, calls=%fused_computation.511 | loop fusion | flops 32563200 | bytes 9913344 | tf_op jit(solution)/shard_map/jvp()/add | solution.py:88
  579.5 13.8 fusion.53
  603.0 14.4 select_reduce_fusion
  655.4 37.4 %all-gather.3.cloned.1.call-done = bf16[3200,768]{1,0:T(8,128)(2,1)} async-done(((bf16[800,768]{1,0:T(8,128)(2,1)}), bf16[3200,768]{1,0:T(8,128)(2,1)}) %all-gather.3.cloned.1.call-update) | async-done | bytes 4915216 | tf_op jit(solution)/shard_map/all_gather | solution.py:200
  704.0 29.5 %all-gather.5.cloned.1.call-done = bf16[3200,768]{1,0:T(8,128)(2,1)} async-done(((bf16[800,768]{1,0:T(8,128)(2,1)}), bf16[3200,768]{1,0:T(8,128)(2,1)}) %all-gather.5.cloned.1.call-update) | async-done | bytes 4915216 | tf_op jit(solution)/shard_map/all_gather | solution.py:211
  789.3 13.9 add_reduce_fusion
  841.3 47.1 %reduce-scatter.3.cloned.1.call-done = bf16[800,768]{1,0:T(8,128)(2,1)} async-done(((bf16[3200,768]{1,0:T(8,128)(2,1)}), bf16[800,768]{1,0:T(8,128)(2,1)}) %reduce-scatter.3.cloned.1.call-update) | async-done | bytes 1228816 | tf_op jit(solution)/shard_map/reduce_scatter | solution.py:205
  899.3 14.3 fusion.57
  913.6 24.3 %fusion.2 = (bf16[1,8,800,1000]{3,2,1,0:T(8,128)(2,1)}, f32[8,800]{1,0:T(8,128)S(1)}) fusion(f32[8,800,1000]{2,1,0:T(8,128)} %get-tuple-element.317, f32[8,800]{1,0:T(8,128)S(1)} %copy-done.77, pred[1000]{0:T(1024)(128)(4,1)S(1)} %copy-done.212, f32[8,800,1000]{2,1,0:T(8,128)} %fusion.57), kind=kLoop, calls=%fused_computation.8 | loop fusion | flops 31993600 | bytes 64052200 | tf_op jit(solution)/shard_map/exp | solution.py:236
  942.5 16.9 multiply_convert_fusion
  993.0 35.6 %multiply_reduce_fusion.62 = (f32[768]{0:T(1024)}, f32[768]{0:T(1024)}, f32[768]{0:T(1024)}, f32[768]{0:T(1024)}, f32[768]{0:T(1024)}, /*index=5*/f32[768]{0:T(1024)}, f32[768]{0:T(1024)}, f32[768]{0:T(1024)}, f32[768]{0:T(1024)}) fusion(f32[1,8,10,10,768]{4,0,3,2,1:T(1,128)} %reshape.3234, f32[1,8,10,10,768]{4,0,3,2,1:T(1,128)} %get-tuple-element.142), kind=kLoop, calls=%fused_computation.166 | loop fusion | flops 11052288 | bytes 4942848 | tf_op jit(solution)/shard_map/transpose(jvp())/reduce_sum | solution.py:88
  1028.7 26.9 %multiply_reduce_fusion.63 = (f32[768]{0:T(1024)}, f32[768]{0:T(1024)}, f32[768]{0:T(1024)}, f32[768]{0:T(1024)}, f32[768]{0:T(1024)}, /*index=5*/f32[768]{0:T(1024)}, f32[768]{0:T(1024)}, f32[768]{0:T(1024)}, f32[768]{0:T(1024)}) fusion(f32[1,8,10,10,768]{4,0,3,2,1:T(1,128)S(1)} %copy-done.2, f32[1,8,10,10,768]{4,0,3,2,1:T(1,128)S(1)} %copy-done.15), kind=kLoop, calls=%fused_computation.167 | loop fusion | flops 11052288 | bytes 4942848 | tf_op jit(solution)/shard_map/transpose(jvp())/reduce_sum | solution.py:88
  1076.0 35.6 %multiply_reduce_fusion.89 = (f32[768]{0:T(1024)}, f32[768]{0:T(1024)}, f32[768]{0:T(1024)}, f32[768]{0:T(1024)}, f32[768]{0:T(1024)}, /*index=5*/f32[768]{0:T(1024)}, f32[768]{0:T(1024)}, f32[768]{0:T(1024)}, f32[768]{0:T(1024)}) fusion(f32[1,8,10,10,768]{4,0,3,2,1:T(1,128)} %reshape.3232, f32[1,8,10,10,768]{4,0,3,2,1:T(1,128)} %copy-done.17), kind=kLoop, calls=%fused_computation.193 | loop fusion | flops 11052288 | bytes 4942848 | tf_op jit(solution)/shard_map/transpose(jvp())/reduce_sum | solution.py:88
  1111.6 26.9 %multiply_reduce_fusion.90 = (f32[768]{0:T(1024)}, f32[768]{0:T(1024)}, f32[768]{0:T(1024)}, f32[768]{0:T(1024)}, f32[768]{0:T(1024)}, /*index=5*/f32[768]{0:T(1024)}, f32[768]{0:T(1024)}, f32[768]{0:T(1024)}, f32[768]{0:T(1024)}) fusion(f32[1,8,10,10,768]{4,0,3,2,1:T(1,128)S(1)} %copy-done.5, f32[1,8,10,10,768]{4,0,3,2,1:T(1,128)S(1)} %copy-done.18), kind=kLoop, calls=%fused_computation.194 | loop fusion | flops 11052288 | bytes 4942848 | tf_op jit(solution)/shard_map/transpose(jvp())/reduce_sum | solution.py:88
  1149.1 26.9 %multiply_reduce_fusion.88 = (f32[768]{0:T(1024)}, f32[768]{0:T(1024)}, f32[768]{0:T(1024)}, f32[768]{0:T(1024)}, f32[768]{0:T(1024)}, /*index=5*/f32[768]{0:T(1...) fusion(f32[1,8,10,10,768]{4,0,3,2,1:T(1,128)} %reshape.3232, ...), kind=kLoop, calls=%fused_computation.192 | loop fusion | flops 11053056 | bytes 9861120 | tf_op jit(solution)/shard_map/transpose(jvp())/reduce_sum | solution.py:88
  1176.1 23.8 %multiply_reduce_fusion.61 = (f32[768]{0:T(1024)}, f32[768]{0:T(1024)}, f32[768]{0:T(1024)}, f32[768]{0:T(1024)}, f32[768]{0:T(1024)}, /*index=5*/f32[768]{0:T(1...) fusion(f32[1,8,10,10,768]{4,0,3,2,1:T(1,128)S(1)} %copy-done.3, ...), kind=kLoop, calls=%fused_computation.165 | loop fusion | flops 11053056 | bytes 9861120 | tf_op jit(solution)/shard_map/transpose(jvp())/reduce_sum | solution.py:88
  1256.4 35.1 %multiply_reduce_fusion.35 = (f32[768]{0:T(1024)S(1)}, f32[768]{0:T(1024)S(1)}, f32[768]{0:T(1024)S(1)}, f32[768]{0:T(1024)S(1)}, f32[768]{0:T(1024)S(1)}, /*ind...) fusion(f32[1,8,10,10,768]{4,0,3,2,1:T(1,128)} %reshape.3237, ...), kind=kLoop, calls=%fused_computation.139 | loop fusion | flops 11052288 | bytes 4942848 | tf_op jit(solution)/shard_map/transpose(jvp())/reduce_sum | solution.py:88
  1291.6 26.3 %multiply_reduce_fusion.36 = (f32[768]{0:T(1024)S(1)}, f32[768]{0:T(1024)S(1)}, f32[768]{0:T(1024)S(1)}, f32[768]{0:T(1024)S(1)}, f32[768]{0:T(1024)S(1)}, /*ind...) fusion(f32[1,8,10,10,768]{4,0,3,2,1:T(1,128)S(1)} %copy-done.11, ...), kind=kLoop, calls=%fused_computation.140 | loop fusion | flops 11052288 | bytes 4942848 | tf_op jit(solution)/shard_map/transpose(jvp())/reduce_sum | solution.py:88
  1318.1 22.0 %multiply_reduce_fusion.34 = (f32[768]{0:T(1024)S(1)}, f32[768]{0:T(1024)S(1)}, f32[768]{0:T(1024)S(1)}, f32[768]{0:T(1024)S(1)}, f32[768]{0:T(1024)S(1)}, /*ind...) fusion(f32[1,8,10,10,768]{4,0,3,2,1:T(1,128)S(1)} %copy-done.11, ...), kind=kLoop, calls=%fused_computation.138 | loop fusion | flops 11053056 | bytes 9861120 | tf_op jit(solution)/shard_map/transpose(jvp())/reduce_sum | solution.py:88
  1362.4 23.0 %multiply_reduce_fusion.77 = (f32[768]{0:T(1024)}, f32[768]{0:T(1024)S(1)}, f32[768]{0:T(1024)S(1)}, f32[1,8,10,10,768]{4,0,3,2,1:T(1,128)S(1)}, f32[1,8,10,10,7...) fusion(f32[1,8,10,10,768]{4,0,3,2,1:T(1,128)S(1)} %copy-done.6,, ...), kind=kLoop, calls=%fused_computation.181 | loop fusion | flops 11671296 | bytes 46743552 | tf_op jit(solution)/shard_map/transpose(jvp())/reduce_sum | solution.py:88
  1385.5 20.5 broadcast_multiply_fusion.27
  1406.4 31.8 %broadcast_multiply_fusion = (f32[1,8,10,10,768]{4,0,3,2,1:T(1,128)}, f32[1,8,10,10,768]{4,0,3,2,1:T(1,128)}, f32[1,8,10,10,768]{4,0,3,2,1:T(1,128)}, f32[1,8,10...) fusion(f32[1,8,10,10,768]{4,0,3,2,1:T(1,128)S(1)} %copy-done.4,, ...), kind=kLoop, calls=%fused_computation.224 | loop fusion | flops 11059200 | bytes 46749696 | tf_op jit(solution)/shard_map/transpose(jvp())/mul | solution.py:88
  1438.4 30.9 %broadcast_multiply_fusion.54 = (f32[1,8,10,10,768]{4,0,3,2,1:T(1,128)}, f32[1,8,10,10,768]{4,0,3,2,1:T(1,128)}, f32[1,8,10,10,768]{4,0,3,2,1:T(1,128)}, f32[1,8...) fusion(f32[1,8,10,10,768]{4,0,3,2,1:T(1,128)S(1)} %copy-done.6,, ...), kind=kLoop, calls=%fused_computation.278 | loop fusion | flops 11059200 | bytes 46749696 | tf_op jit(solution)/shard_map/transpose(jvp())/mul | solution.py:88
  1482.6 60.1 %pad_add_fusion.1 = f32[1,10,12,12,768]{4,0,3,2,1:T(1,128)S(1)} fusion(f32[1,8,10,10,768]{4,0,3,2,1:T(1,128)S(1)} %get-tuple-element.155, f32[1,8,10,10,768]{4,0,3,2,1:T(1,128)S(1)} %get-tuple-element.156, f32[1,8,10,10,768]{4,0,3,2,1:T(1,128)S(1)} %get-tuple-element.157, f32[1,8,10,10,768]{4,0,3,2,1:T(1,128)S(1)} %copy-done.37, ...), kind=kLoop, calls=%fused_computation.30 | loop fusion | flops 22118400 | bytes 56033280 | tf_op jit(solution)/shard_map/transpose(jvp())/add_any | solution.py:81
  1549.2 61.8 %pad_add_fusion.2 = f32[1,10,12,12,768]{4,0,3,2,1:T(1,128)S(1)} fusion(f32[1,8,10,10,768]{4,0,3,2,1:T(1,128)} %get-tuple-element.194, f32[1,8,10,10,768]{4,0,3,2,1:T(1,128)} %get-tuple-element.195, f32[1,8,10,10,768]{4,0,3,2,1:T(1,128)} %get-tuple-element.196, f32[1,8,10,10,768]{4,0,3,2,1:T(1,128)} %get-tuple-element.197, ...), kind=kLoop, calls=%fused_computation.31 | loop fusion | flops 22118400 | bytes 56033280 | tf_op jit(solution)/shard_map/transpose(jvp())/add_any | solution.py:81
  1617.5 61.5 %pad_add_fusion.3 = f32[1,10,12,12,768]{4,0,3,2,1:T(1,128)S(1)} fusion(f32[1,8,10,10,768]{4,0,3,2,1:T(1,128)} %get-tuple-element.169, f32[1,8,10,10,768]{4,0,3,2,1:T(1,128)} %get-tuple-element.170, f32[1,8,10,10,768]{4,0,3,2,1:T(1,128)} %get-tuple-element.171, f32[1,8,10,10,768]{4,0,3,2,1:T(1,128)} %get-tuple-element.172, ...), kind=kLoop, calls=%fused_computation.32 | loop fusion | flops 22118400 | bytes 56033280 | tf_op jit(solution)/shard_map/transpose(jvp())/add_any | solution.py:81
  1778.4 22.1 %psum.125 = f32[768]{0:T(1024)} all-reduce(f32[768]{0:T(1024)S(1)} %copy-done.227), channel_id=1, replica_groups=mesh['dp'=8,'tensor'=4] {'dp'}, use_global_device_ids=true, to_apply=%region_135.136 | all-reduce | flops 768 | bytes 6144 | tf_op jit(solution)/shard_map/psum | solution.py:282
  1800.5 100.9 %all-reduce.187.cloned.1.call-done = (f32[768]{0:T(1024)}, f32[768]{0:T(1024)}, f32[2304]{0:T(1024)}, f32[3,27,96]{2,1,0:T(8,128)}, f32[3,96]{1,0:T(4,128)}, /*i...) async-done(((f32[768]{0:T(1024)}, f32[768]{0:T(1024)}, f32[2304]{0:T(1024)}, ...) | async-done | bytes 81424 | tf_op jit(solution)/shard_map/psum | solution.py:264
  1901.4 197.9 %all-reduce.189.cloned.1.call-done = (f32[768,2304]{1,0:T(8,128)}, f32[768,768]{1,0:T(8,128)}) async-done(((f32[768,2304]{1,0:T(8,128)}, f32[768,768]{1,0:T(8,128)}), (f32[768,2304]{1,0:T(8,128)}, f32[768,768]{1,0:T(8,128)})) %all-reduce.189.cloned.1.call-update) | async-done | bytes 9437200 | tf_op jit(solution)/shard_map/psum | solution.py:264
  (940 shorter events, 788.6 us)
Async XLA Ops:
  7.2 81.0 %copy-start = (bf16[768,2304]{1,0:T(8,128)(2,1)S(1)}, bf16[768,2304]{1,0:T(8,128)(2,1)}, u32[]{:S(2)}) copy-start(bf16[768,2304]{1,0:T(8,128)(2,1)} %param.25) | copy-start | bytes 10616836
  7.2 685.6 %all-gather.3.cloned.1.call-start = ((), (), s32[]{:S(2)}) async-start(), calls=%async_computation.2 | async-start | bytes 6144000 | tf_op jit(solution)/shard_map/all_gather | solution.py:200
  9.3 884.1 %copy-start.87 = (f32[800]{0:T(1024)}, f32[800]{0:T(1024)S(1)}, u32[]{:S(2)}) copy-start(f32[800]{0:T(1024)S(1)} %or_convert_fusion.1) | copy-start | bytes 9604
  21.0 102.9 %copy-start.100 = (f32[768]{0:T(1024)}, f32[768]{0:T(1024)S(1)}, u32[]{:S(2)}) copy-start(f32[768]{0:T(1024)S(1)} %tile.345) | copy-start | bytes 9220
  24.6 71.2 %copy-start.89 = (f32[800]{0:T(1024)}, f32[800]{0:T(1024)S(1)}, u32[]{:S(2)}) copy-start(f32[800]{0:T(1024)S(1)} %broadcast_multiply_fusion.85) | copy-start | bytes 9604
  27.0 68.8 %copy-start.98 = (f32[800]{0:T(1024)}, f32[800]{0:T(1024)S(1)}, u32[]{:S(2)}) copy-start(f32[800]{0:T(1024)S(1)} %fusion.91) | copy-start | bytes 9604
  205.3 139.0 %copy-start.138 = (f32[768]{0:T(1024)}, f32[768]{0:T(1024)S(1)}, u32[]{:S(2)}) copy-start(f32[768]{0:T(1024)S(1)} %tile.497) | copy-start | bytes 9220
  206.7 137.6 %copy-start.140 = (f32[768]{0:T(1024)}, f32[768]{0:T(1024)S(1)}, u32[]{:S(2)}) copy-start(f32[768]{0:T(1024)S(1)} %tile.457) | copy-start | bytes 9220
  208.7 135.5 %copy-start.142 = (f32[768]{0:T(1024)}, f32[768]{0:T(1024)S(1)}, u32[]{:S(2)}) copy-start(f32[768]{0:T(1024)S(1)} %tile.455) | copy-start | bytes 9220
  355.1 141.0 %copy-start.181 = (f32[768]{0:T(1024)}, f32[768]{0:T(1024)S(1)}, u32[]{:S(2)}) copy-start(f32[768]{0:T(1024)S(1)} %tile.421) | copy-start | bytes 9220
  355.8 140.3 %copy-start.183 = (f32[768]{0:T(1024)}, f32[768]{0:T(1024)S(1)}, u32[]{:S(2)}) copy-start(f32[768]{0:T(1024)S(1)} %tile.419) | copy-start | bytes 9220
  357.8 138.3 %copy-start.185 = (f32[768]{0:T(1024)}, f32[768]{0:T(1024)S(1)}, u32[]{:S(2)}) copy-start(f32[768]{0:T(1024)S(1)} %tile.417) | copy-start | bytes 9220
  508.1 120.5 %copy-start.208 = (f32[96]{0:T(128)}, f32[96]{0:T(128)S(1)}, u32[]{:S(2)}) copy-start(f32[96]{0:T(128)S(1)} %get-tuple-element.312) | copy-start | bytes 1156
  651.4 82.2 %all-gather.5.cloned.1.call-start = ((), (), s32[]{:S(2)}) async-start(), calls=%async_computation.4 | async-start | bytes 6144000 | tf_op jit(solution)/shard_map/all_gather | solution.py:211
  654.0 182.7 %reduce-scatter.5.cloned.1.call-start = ((), (), s32[]{:S(2)}) async-start(), calls=%async_computation.5 | async-start | bytes 12288000 | tf_op jit(solution)/shard_map/reduce_scatter | solution.py:219
  755.6 132.8 %reduce-scatter.3.cloned.1.call-start = ((), (), s32[]{:S(2)}) async-start(), calls=%async_computation.3 | async-start | bytes 6144000 | tf_op jit(solution)/shard_map/reduce_scatter | solution.py:205
  765.6 1034.9 %all-reduce.191.cloned.1.call-start = ((), (), s32[]{:S(2)}) async-start(), calls=%async_computation.8 | async-start | bytes 9437184 | tf_op jit(solution)/shard_map/psum | solution.py:282
  830.1 1071.3 %all-reduce.187.cloned.1.call-start = ((), (), s32[]{:S(2)}) async-start(), calls=%async_computation.6 | async-start | bytes 237568 | tf_op jit(solution)/shard_map/psum | solution.py:264
  1549.1 136.4 %copy-start.24 = (f32[1,1,8,10,10,768]{5,0,4,3,2,1:T(1,128)}, f32[1,1,8,10,10,768]{5,0,4,3,2,1:T(1,128)S(1)}, u32[]{:S(2)}) copy-start(f32[1,1,8,10,10,768]{5,0,4,3,2,1:T(1,128)S(1)} %fusion.37) | copy-start | bytes 7372804
  1549.1 61.9 %copy-start.35 = (f32[1,8,10,10,768]{4,0,3,2,1:T(1,128)S(1)}, f32[1,8,10,10,768]{4,0,3,2,1:T(1,128)}, u32[]{:S(2)}) copy-start(f32[1,8,10,10,768]{4,0,3,2,1:T(1,128)} %get-tuple-element.147) | copy-start | bytes 7372804
  1549.1 61.9 %copy-start.36 = (f32[1,8,10,10,768]{4,0,3,2,1:T(1,128)S(1)}, f32[1,8,10,10,768]{4,0,3,2,1:T(1,128)}, u32[]{:S(2)}) copy-start(f32[1,8,10,10,768]{4,0,3,2,1:T(1,128)} %get-tuple-element.148) | copy-start | bytes 7372804
  1549.1 61.9 %copy-start.38 = (f32[1,8,10,10,768]{4,0,3,2,1:T(1,128)S(1)}, f32[1,8,10,10,768]{4,0,3,2,1:T(1,128)}, u32[]{:S(2)}) copy-start(f32[1,8,10,10,768]{4,0,3,2,1:T(1,128)} %get-tuple-element.190) | copy-start | bytes 7372804
  1549.1 61.9 %copy-start.39 = (f32[1,8,10,10,768]{4,0,3,2,1:T(1,128)S(1)}, f32[1,8,10,10,768]{4,0,3,2,1:T(1,128)}, u32[]{:S(2)}) copy-start(f32[1,8,10,10,768]{4,0,3,2,1:T(1,128)} %get-tuple-element.191) | copy-start | bytes 7372804
  1549.2 61.9 %copy-start.40 = (f32[1,8,10,10,768]{4,0,3,2,1:T(1,128)S(1)}, f32[1,8,10,10,768]{4,0,3,2,1:T(1,128)}, u32[]{:S(2)}) copy-start(f32[1,8,10,10,768]{4,0,3,2,1:T(1,128)} %get-tuple-element.192) | copy-start | bytes 7372804
  1549.2 61.9 %copy-start.41 = (f32[1,8,10,10,768]{4,0,3,2,1:T(1,128)S(1)}, f32[1,8,10,10,768]{4,0,3,2,1:T(1,128)}, u32[]{:S(2)}) copy-start(f32[1,8,10,10,768]{4,0,3,2,1:T(1,128)} %get-tuple-element.193) | copy-start | bytes 7372804
  1617.4 68.0 %copy-start.25 = (f32[1,1,8,10,10,768]{5,0,4,3,2,1:T(1,128)}, f32[1,1,8,10,10,768]{5,0,4,3,2,1:T(1,128)S(1)}, u32[]{:S(2)}) copy-start(f32[1,1,8,10,10,768]{5,0,4,3,2,1:T(1,128)S(1)} %fusion.38) | copy-start | bytes 7372804
  1617.5 61.5 %copy-start.33 = (f32[1,8,10,10,768]{4,0,3,2,1:T(1,128)S(1)}, f32[1,8,10,10,768]{4,0,3,2,1:T(1,128)}, u32[]{:S(2)}) copy-start(f32[1,8,10,10,768]{4,0,3,2,1:T(1,128)} %get-tuple-element.145) | copy-start | bytes 7372804
  1617.5 61.5 %copy-start.34 = (f32[1,8,10,10,768]{4,0,3,2,1:T(1,128)S(1)}, f32[1,8,10,10,768]{4,0,3,2,1:T(1,128)}, u32[]{:S(2)}) copy-start(f32[1,8,10,10,768]{4,0,3,2,1:T(1,128)} %get-tuple-element.146) | copy-start | bytes 7372804
  1617.5 61.5 %copy-start.42 = (f32[1,8,10,10,768]{4,0,3,2,1:T(1,128)S(1)}, f32[1,8,10,10,768]{4,0,3,2,1:T(1,128)}, u32[]{:S(2)}) copy-start(f32[1,8,10,10,768]{4,0,3,2,1:T(1,128)} %get-tuple-element.165) | copy-start | bytes 7372804
  1617.5 61.5 %copy-start.43 = (f32[1,8,10,10,768]{4,0,3,2,1:T(1,128)S(1)}, f32[1,8,10,10,768]{4,0,3,2,1:T(1,128)}, u32[]{:S(2)}) copy-start(f32[1,8,10,10,768]{4,0,3,2,1:T(1,128)} %get-tuple-element.166) | copy-start | bytes 7372804
  1617.5 61.5 %copy-start.44 = (f32[1,8,10,10,768]{4,0,3,2,1:T(1,128)S(1)}, f32[1,8,10,10,768]{4,0,3,2,1:T(1,128)}, u32[]{:S(2)}) copy-start(f32[1,8,10,10,768]{4,0,3,2,1:T(1,128)} %get-tuple-element.167) | copy-start | bytes 7372804
  1772.2 327.1 %all-reduce.189.cloned.1.call-start = ((), (), s32[]{:S(2)}) async-start(), calls=%async_computation.7 | async-start | bytes 18874368 | tf_op jit(solution)/shard_map/psum | solution.py:264
  (229 other events, 3376.2 us)
Sparse Core Ops, SparseCore 0:
  651.5 41.2 all-gather.2
  694.9 38.5 all-gather.4
  755.7 80.9 reduce-scatter.4
  839.2 49.1 reduce-scatter.2
  892.9 169.9 all-reduce.190
  1772.3 129.0 all-reduce.186
  1908.5 190.7 all-reduce.188
where the time goes:
time: 2140 us; the launch traced here: 2130 us
  other arithmetic  1000 us (47%)
  local copies, waits for them, and re-layouts  457 us (21%)
  waiting for transfers between devices  420 us (20%)
  matrix products  205 us (10%)
  blocking collectives  22.1 us (1%)
    psum x2, waiting for transfers between devices, per_device(): lax.psum((grad_from_one[1], grad_from_one[2], grad_w_qkv, grad_b_qkv, poo...  299 us
    reduce_sum x10, other arithmetic, pool_field(): accumulated = accumulated + window * kernel_wide[kernel_tap]  282 us
    add x3, other arithmetic, pool_field(): accumulated = accumulated + window * kernel_wide[kernel_tap]  221 us
    another operation x162, local copies, waits for them, and re-layouts, pool_field(): kernel_wide = jnp.tile(kernel, (1, HEADS))  191 us
    add_any x3, other arithmetic, pool_field(): padded[:, frame_shift:frame_shift + FRAMES, row_shift:row_shift + SIDE, c...  183 us
    mul x5, other arithmetic, pool_field(): accumulated = accumulated + window * kernel_wide[kernel_tap]  105 us
    reshape x10, local copies, waits for them, and re-layouts, pool_norm(): per_head = pooled.reshape(clip_count, LENGTH, HEADS, HEAD_DIM)  54.4 us
    reduce_scatter x1, waiting for transfers between devices, per_device(): lax.psum_scatter(jnp.dot(row_piece, w_down, preferred_element_type=jnp.fl...  47.1 us
  transfers between devices with their start and end apart: 7, of which 6 were waited for; matrix products, arithmetic and copies ran while one was open for 46% of the time, Pallas kernels for 0%

commit v1 on v0

--- a/solution.py
+++ b/solution.py
@@ -262,22 +262,25 @@
     grad_from_one = norm_one_back(grad_normed_one)
     input_grad = grad_middle + grad_from_one[0]
     summed = lax.psum(
-        (
-            grad_from_one[1],
-            grad_from_one[2],
-            grad_w_qkv,
-            grad_b_qkv,
-            pool_grads[1],
-            pool_grads[2],
-            pool_grads[3],
-            offset_grads[1],
-            grad_w_proj,
-            grad_b_proj,
-            grad_from_two[1],
-            grad_from_two[2],
-            grad_b_down,
+        lax.psum(
+            (
+                grad_from_one[1],
+                grad_from_one[2],
+                grad_w_qkv,
+                grad_b_qkv,
+                pool_grads[1],
+                pool_grads[2],
+                pool_grads[3],
+                offset_grads[1],
+                grad_w_proj,
+                grad_b_proj,
+                grad_from_two[1],
+                grad_from_two[2],
+                grad_b_down,
+            ),
+            "tensor",
         ),
-        ("dp", "tensor"),
+        "dp",
     )
     mlp_summed = lax.psum((grad_w_up, grad_b_up, grad_w_down), "dp")
     return (

time: 2140 us -> 2550 us (1.19)
  waiting for transfers between devices: 420 us -> 846 us
    psum x1 -> x2, waiting for transfers between devices: 0.01 us -> 524 us  [per_device(): lax.psum(lax.psum((grad_from_one[1], grad_from_one[2], grad_w_qkv, grad_b...]
    psum x2, waiting for transfers between devices: 299 us -> 182 us  [per_device(): lax.psum((grad_from_one[1], grad_from_one[2], grad_w_qkv, grad_b_qkv, poo...]
  transfers between devices with their start and end apart: 7 -> 8, of which waited for: 6 -> 8; matrix products, arithmetic and copies ran while one was open for 46% -> 4% of each run, Pallas kernels for 0% -> 0%
where the time goes in v1:
time: 2550 us; the launch traced here: 2540 us
  other arithmetic  1010 us (40%)
  waiting for transfers between devices  846 us (33%)
  local copies, waits for them, and re-layouts  454 us (18%)
  matrix products  210 us (8%)
    psum x2, waiting for transfers between devices, per_device(): lax.psum(lax.psum((grad_from_one[1], grad_from_one[2], grad_w_qkv, grad_b...  524 us
    reduce_sum x10, other arithmetic, pool_field(): accumulated = accumulated + window * kernel_wide[kernel_tap]  283 us
    add x3, other arithmetic, pool_field(): accumulated = accumulated + window * kernel_wide[kernel_tap]  222 us
    another operation x162, local copies, waits for them, and re-layouts, pool_field(): kernel_wide = jnp.tile(kernel, (1, HEADS))  190 us
    add_any x3, other arithmetic, pool_field(): padded[:, frame_shift:frame_shift + FRAMES, row_shift:row_shift + SIDE, c...  184 us
    psum x2, waiting for transfers between devices, per_device(): lax.psum((grad_from_one[1], grad_from_one[2], grad_w_qkv, grad_b_qkv, poo...  182 us
    mul x5, other arithmetic, pool_field(): accumulated = accumulated + window * kernel_wide[kernel_tap]  105 us
    reshape x10, local copies, waits for them, and re-layouts, pool_norm(): per_head = pooled.reshape(clip_count, LENGTH, HEADS, HEAD_DIM)  54.4 us
  transfers between devices with their start and end apart: 8, of which 8 were waited for; matrix products, arithmetic and copies ran while one was open for 4% of the time, Pallas kernels for 0%

profile of v1, /device:TPU:0, one launch (start us, length us, event | category | flops | bytes accessed | tf_op | source)
XLA Modules:
  0.0 2543.2 jit_solution(4869420801762791247)
XLA Ops:
  108.4 15.2 slice_bitcast_fusion.7
  125.2 69.1 %add_reduce_fusion.2 = f32[8,10,10,768]{3,2,1,0:T(8,128)} fusion(f32[768]{0:T(1024)S(1)} %copy-done.109, f32[768]{0:T(1024)S(1)} %copy-done.137, f32[768]{0:T(1024)S(1)} %copy-done.145, f32[768]{0:T(1024)S(1)} %copy-done.148, f32[768]{0:T(1024)S(1)} %copy-done.151, f32[768]{0:T(1024)S(1)} %copy-done.154, f32[768]{0:T(1024)S(1)} %copy-done.156, ...), kind=kLoop, calls=%fused_computation.210 | loop fusion | flops 32563200 | bytes 7455744 | tf_op jit(solution)/shard_map/jvp()/add | solution.py:88
  267.7 76.4 %add_reduce_fusion.1 = f32[8,10,10,768]{3,2,1,0:T(8,128)} fusion(f32[768]{0:T(1024)S(1)} %tile.497, f32[768]{0:T(1024)} %tile.495, f32[768]{0:T(1024)} %tile.493, f32[768]{0:T(1024)} %tile.491, f32[768]{0:T(1024)} %tile.489, f32[768]{0:T(1024)} %tile.487, f32[768]{0:T(1024)} %tile.485, f32[768]{0:T(1024)} %tile.483, f32[768]{0:T(1024)} %tile.481, ...), kind=kLoop, calls=%fused_computation.208 | loop fusion | flops 32563200 | bytes 7455744 | tf_op jit(solution)/shard_map/jvp()/add | solution.py:88
  419.3 76.2 %fusion.116 = (f32[8,10,10,768]{3,2,1,0:T(8,128)}, f32[1,8,10,10,768]{4,0,3,2,1:T(1,128)}) fusion(f32[768]{0:T(1024)} %tile.443, f32[768]{0:T(1024)} %tile.441, f32[768]{0:T(1024)} %tile.439, f32[768]{0:T(1024)} %tile.437, f32[768]{0:T(1024)} %tile.435, f32[768]{0:T(1024)} %tile.433, f32[768]{0:T(1024)} %tile.431, f32[768]{0:T(1024)} %tile.429, ...), kind=kLoop, calls=%fused_computation.511 | loop fusion | flops 32563200 | bytes 9913344 | tf_op jit(solution)/shard_map/jvp()/add | solution.py:88
  602.1 14.5 select_reduce_fusion
  654.7 37.4 %all-gather.3.cloned.1.call-done = bf16[3200,768]{1,0:T(8,128)(2,1)} async-done(((bf16[800,768]{1,0:T(8,128)(2,1)}), bf16[3200,768]{1,0:T(8,128)(2,1)}) %all-gather.3.cloned.1.call-update) | async-done | bytes 4915216 | tf_op jit(solution)/shard_map/all_gather | solution.py:200
  703.4 29.5 %all-gather.5.cloned.1.call-done = bf16[3200,768]{1,0:T(8,128)(2,1)} async-done(((bf16[800,768]{1,0:T(8,128)(2,1)}), bf16[3200,768]{1,0:T(8,128)(2,1)}) %all-gather.5.cloned.1.call-update) | async-done | bytes 4915216 | tf_op jit(solution)/shard_map/all_gather | solution.py:211
  810.5 25.5 %reduce-scatter.5.cloned.1.call-done = f32[800,768]{1,0:T(8,128)} async-done(((f32[3200,768]{1,0:T(8,128)}), f32[800,768]{1,0:T(8,128)}) %reduce-scatter.5.cloned.1.call-update) | async-done | bytes 2457616 | tf_op jit(solution)/shard_map/reduce_scatter | solution.py:219
  840.7 47.7 %reduce-scatter.3.cloned.1.call-done = bf16[800,768]{1,0:T(8,128)(2,1)} async-done(((bf16[3200,768]{1,0:T(8,128)(2,1)}), bf16[800,768]{1,0:T(8,128)(2,1)}) %reduce-scatter.3.cloned.1.call-update) | async-done | bytes 1228816 | tf_op jit(solution)/shard_map/reduce_scatter | solution.py:205
  899.1 14.1 fusion.57
  913.2 24.4 fusion.2
  941.5 17.3 multiply_convert_fusion
  992.0 35.9 %multiply_reduce_fusion.62 = (f32[768]{0:T(1024)}, f32[768]{0:T(1024)}, f32[768]{0:T(1024)}, f32[768]{0:T(1024)}, f32[768]{0:T(1024)}, /*index=5*/f32[768]{0:T(1024)}, f32[768]{0:T(1024)}, f32[768]{0:T(1024)}, f32[768]{0:T(1024)}) fusion(f32[1,8,10,10,768]{4,0,3,2,1:T(1,128)} %reshape.3234, f32[1,8,10,10,768]{4,0,3,2,1:T(1,128)} %get-tuple-element.156), kind=kLoop, calls=%fused_computation.166 | loop fusion | flops 11052288 | bytes 4942848 | tf_op jit(solution)/shard_map/transpose(jvp())/reduce_sum | solution.py:88
  1028.0 26.9 %multiply_reduce_fusion.63 = (f32[768]{0:T(1024)}, f32[768]{0:T(1024)}, f32[768]{0:T(1024)}, f32[768]{0:T(1024)}, f32[768]{0:T(1024)}, /*index=5*/f32[768]{0:T(1024)}, f32[768]{0:T(1024)}, f32[768]{0:T(1024)}, f32[768]{0:T(1024)}) fusion(f32[1,8,10,10,768]{4,0,3,2,1:T(1,128)S(1)} %copy-done.2, f32[1,8,10,10,768]{4,0,3,2,1:T(1,128)S(1)} %copy-done.16), kind=kLoop, calls=%fused_computation.167 | loop fusion | flops 11052288 | bytes 4942848 | tf_op jit(solution)/shard_map/transpose(jvp())/reduce_sum | solution.py:88
  1083.0 35.7 %multiply_reduce_fusion.89 = (f32[768]{0:T(1024)}, f32[768]{0:T(1024)}, f32[768]{0:T(1024)}, f32[768]{0:T(1024)}, f32[768]{0:T(1024)}, /*index=5*/f32[768]{0:T(1024)}, f32[768]{0:T(1024)}, f32[768]{0:T(1024)}, f32[768]{0:T(1024)}) fusion(f32[1,8,10,10,768]{4,0,3,2,1:T(1,128)} %reshape.3232, f32[1,8,10,10,768]{4,0,3,2,1:T(1,128)} %copy-done.18), kind=kLoop, calls=%fused_computation.193 | loop fusion | flops 11052288 | bytes 4942848 | tf_op jit(solution)/shard_map/transpose(jvp())/reduce_sum | solution.py:88
  1118.7 27.1 %multiply_reduce_fusion.90 = (f32[768]{0:T(1024)}, f32[768]{0:T(1024)}, f32[768]{0:T(1024)}, f32[768]{0:T(1024)}, f32[768]{0:T(1024)}, /*index=5*/f32[768]{0:T(1024)}, f32[768]{0:T(1024)}, f32[768]{0:T(1024)}, f32[768]{0:T(1024)}) fusion(f32[1,8,10,10,768]{4,0,3,2,1:T(1,128)S(1)} %copy-done.5, f32[1,8,10,10,768]{4,0,3,2,1:T(1,128)S(1)} %copy-done.19), kind=kLoop, calls=%fused_computation.194 | loop fusion | flops 11052288 | bytes 4942848 | tf_op jit(solution)/shard_map/transpose(jvp())/reduce_sum | solution.py:88
  1156.4 26.9 %multiply_reduce_fusion.88 = (f32[768]{0:T(1024)}, f32[768]{0:T(1024)}, f32[768]{0:T(1024)}, f32[768]{0:T(1024)}, f32[768]{0:T(1024)}, /*index=5*/f32[768]{0:T(1...) fusion(f32[1,8,10,10,768]{4,0,3,2,1:T(1,128)} %reshape.3232, ...), kind=kLoop, calls=%fused_computation.192 | loop fusion | flops 11053056 | bytes 9861120 | tf_op jit(solution)/shard_map/transpose(jvp())/reduce_sum | solution.py:88
  1183.4 23.8 multiply_reduce_fusion.61
  1263.7 35.8 %multiply_reduce_fusion.35 = (f32[768]{0:T(1024)}, f32[768]{0:T(1024)}, f32[768]{0:T(1024)}, f32[768]{0:T(1024)}, f32[768]{0:T(1024)}, /*index=5*/f32[768]{0:T(1024)}, f32[768]{0:T(1024)}, f32[768]{0:T(1024)}, f32[768]{0:T(1024)}) fusion(f32[1,8,10,10,768]{4,0,3,2,1:T(1,128)} %reshape.3237, f32[1,8,10,10,768]{4,0,3,2,1:T(1,128)} %get-tuple-element.157), kind=kLoop, calls=%fused_computation.139 | loop fusion | flops 11052288 | bytes 4942848 | tf_op jit(solution)/shard_map/transpose(jvp())/reduce_sum | solution.py:88
  1299.5 26.9 %multiply_reduce_fusion.36 = (f32[768]{0:T(1024)}, f32[768]{0:T(1024)}, f32[768]{0:T(1024)}, f32[768]{0:T(1024)}, f32[768]{0:T(1024)}, /*index=5*/f32[768]{0:T(1024)}, f32[768]{0:T(1024)}, f32[768]{0:T(1024)}, f32[768]{0:T(1024)}) fusion(f32[1,8,10,10,768]{4,0,3,2,1:T(1,128)S(1)} %copy-done.11, f32[1,8,10,10,768]{4,0,3,2,1:T(1,128)S(1)} %copy-done.15), kind=kLoop, calls=%fused_computation.140 | loop fusion | flops 11052288 | bytes 4942848 | tf_op jit(solution)/shard_map/transpose(jvp())/reduce_sum | solution.py:88
  1326.5 22.0 multiply_reduce_fusion.34
  1370.8 22.4 multiply_reduce_fusion.77
  1393.4 20.5 broadcast_multiply_fusion.27
  1414.3 31.8 %broadcast_multiply_fusion = (f32[1,8,10,10,768]{4,0,3,2,1:T(1,128)}, f32[1,8,10,10,768]{4,0,3,2,1:T(1,128)}, f32[1,8,10,10,768]{4,0,3,2,1:T(1,128)}, f32[1,8,10...) fusion(f32[1,8,10,10,768]{4,0,3,2,1:T(1,128)S(1)} %copy-done.4,, ...), kind=kLoop, calls=%fused_computation.224 | loop fusion | flops 11059200 | bytes 46749696 | tf_op jit(solution)/shard_map/transpose(jvp())/mul | solution.py:88
  1446.2 31.0 %broadcast_multiply_fusion.54 = (f32[1,8,10,10,768]{4,0,3,2,1:T(1,128)}, f32[1,8,10,10,768]{4,0,3,2,1:T(1,128)}, f32[1,8,10,10,768]{4,0,3,2,1:T(1,128)}, f32[1,8...) fusion(f32[1,8,10,10,768]{4,0,3,2,1:T(1,128)S(1)} %copy-done.6,, ...), kind=kLoop, calls=%fused_computation.278 | loop fusion | flops 11059200 | bytes 46749696 | tf_op jit(solution)/shard_map/transpose(jvp())/mul | solution.py:88
  1477.2 60.1 %pad_add_fusion.1 = f32[1,10,12,12,768]{4,0,3,2,1:T(1,128)S(1)} fusion(f32[1,8,10,10,768]{4,0,3,2,1:T(1,128)S(1)} %get-tuple-element.169, f32[1,8,10,10,768]{4,0,3,2,1:T(1,128)S(1)} %get-tuple-element.170, f32[1,8,10,10,768]{4,0,3,2,1:T(1,128)S(1)} %get-tuple-element.171, f32[1,8,10,10,768]{4,0,3,2,1:T(1,128)S(1)} %copy-done.38, ...), kind=kLoop, calls=%fused_computation.30 | loop fusion | flops 22118400 | bytes 56033280 | tf_op jit(solution)/shard_map/transpose(jvp())/add_any | solution.py:81
  1543.8 62.1 %pad_add_fusion.2 = f32[1,10,12,12,768]{4,0,3,2,1:T(1,128)S(1)} fusion(f32[1,8,10,10,768]{4,0,3,2,1:T(1,128)} %get-tuple-element.208, f32[1,8,10,10,768]{4,0,3,2,1:T(1,128)} %get-tuple-element.209, f32[1,8,10,10,768]{4,0,3,2,1:T(1,128)} %get-tuple-element.210, f32[1,8,10,10,768]{4,0,3,2,1:T(1,128)} %get-tuple-element.211, ...), kind=kLoop, calls=%fused_computation.31 | loop fusion | flops 22118400 | bytes 56033280 | tf_op jit(solution)/shard_map/transpose(jvp())/add_any | solution.py:81
  1612.4 61.8 %pad_add_fusion.3 = f32[1,10,12,12,768]{4,0,3,2,1:T(1,128)S(1)} fusion(f32[1,8,10,10,768]{4,0,3,2,1:T(1,128)} %get-tuple-element.183, f32[1,8,10,10,768]{4,0,3,2,1:T(1,128)} %get-tuple-element.184, f32[1,8,10,10,768]{4,0,3,2,1:T(1,128)} %get-tuple-element.185, f32[1,8,10,10,768]{4,0,3,2,1:T(1,128)} %get-tuple-element.186, ...), kind=kLoop, calls=%fused_computation.32 | loop fusion | flops 22118400 | bytes 56033280 | tf_op jit(solution)/shard_map/transpose(jvp())/add_any | solution.py:81
  1801.1 16.6 all-reduce.193.cloned.1.call-done
  1827.2 165.0 %all-reduce.195.cloned.1.call-done = (f32[768,2304]{1,0:T(8,128)}, f32[768,768]{1,0:T(8,128)}) async-done(((f32[768,2304]{1,0:T(8,128)}, f32[768,768]{1,0:T(8,128)}), (f32[768,2304]{1,0:T(8,128)}, f32[768,768]{1,0:T(8,128)})) %all-reduce.195.cloned.1.call-update) | async-done | bytes 9437200 | tf_op jit(solution)/shard_map/psum | solution.py:265
  1992.2 78.1 %all-reduce.189.cloned.1.call-done = (f32[768]{0:T(1024)}, f32[768]{0:T(1024)}, f32[2304]{0:T(1024)}, f32[3,27,96]{2,1,0:T(8,128)}, f32[3,96]{1,0:T(4,128)}, /*i...) async-done(((f32[768]{0:T(1024)}, f32[768]{0:T(1024)}, f32[2304]{0:T(1024)}, ...) | async-done | bytes 84496 | tf_op jit(solution)/shard_map/psum | solution.py:264
  2070.3 446.4 %all-reduce.191.cloned.1.call-done = (f32[768,2304]{1,0:T(8,128)}, f32[768,768]{1,0:T(8,128)}, f32[768,768]{1,0:T(8,128)}, f32[768,768]{1,0:T(8,128)}) async-done(((f32[768,2304]{1,0:T(8,128)}, f32[768,768]{1,0:T(8,128)}, f32[768,768]{1,0:T(8,128)}, f32[768,768]{1,0:T(8,128)}), (f32[768,2304]{1,0:T(8,128)}, f32[768,768]{1,0:T(8,128)}, f32[768,768]{1,0:T(8,128)}, ...) | async-done | bytes 14155792 | tf_op jit(solution)/shard_map/psum | solution.py:264
  (1035 shorter events, 820.2 us)
Async XLA Ops:
  7.2 80.9 %copy-start = (bf16[768,2304]{1,0:T(8,128)(2,1)S(1)}, bf16[768,2304]{1,0:T(8,128)(2,1)}, u32[]{:S(2)}) copy-start(bf16[768,2304]{1,0:T(8,128)(2,1)} %param.25) | copy-start | bytes 10616836
  7.2 684.9 %all-gather.3.cloned.1.call-start = ((), (), s32[]{:S(2)}) async-start(), calls=%async_computation.2 | async-start | bytes 6144000 | tf_op jit(solution)/shard_map/all_gather | solution.py:200
  9.3 884.1 %copy-start.88 = (f32[800]{0:T(1024)}, f32[800]{0:T(1024)S(1)}, u32[]{:S(2)}) copy-start(f32[800]{0:T(1024)S(1)} %or_convert_fusion.1) | copy-start | bytes 9604
  21.0 102.5 %copy-start.101 = (f32[768]{0:T(1024)}, f32[768]{0:T(1024)S(1)}, u32[]{:S(2)}) copy-start(f32[768]{0:T(1024)S(1)} %tile.345) | copy-start | bytes 9220
  24.6 71.0 %copy-start.90 = (f32[800]{0:T(1024)}, f32[800]{0:T(1024)S(1)}, u32[]{:S(2)}) copy-start(f32[800]{0:T(1024)S(1)} %broadcast_multiply_fusion.85) | copy-start | bytes 9604
  27.0 68.6 %copy-start.99 = (f32[800]{0:T(1024)}, f32[800]{0:T(1024)S(1)}, u32[]{:S(2)}) copy-start(f32[800]{0:T(1024)S(1)} %fusion.91) | copy-start | bytes 9604
  205.0 139.1 %copy-start.139 = (f32[768]{0:T(1024)}, f32[768]{0:T(1024)S(1)}, u32[]{:S(2)}) copy-start(f32[768]{0:T(1024)S(1)} %tile.497) | copy-start | bytes 9220
  206.4 137.7 %copy-start.141 = (f32[768]{0:T(1024)}, f32[768]{0:T(1024)S(1)}, u32[]{:S(2)}) copy-start(f32[768]{0:T(1024)S(1)} %tile.457) | copy-start | bytes 9220
  208.4 135.7 %copy-start.143 = (f32[768]{0:T(1024)}, f32[768]{0:T(1024)S(1)}, u32[]{:S(2)}) copy-start(f32[768]{0:T(1024)S(1)} %tile.455) | copy-start | bytes 9220
  354.9 140.5 %copy-start.182 = (f32[768]{0:T(1024)}, f32[768]{0:T(1024)S(1)}, u32[]{:S(2)}) copy-start(f32[768]{0:T(1024)S(1)} %tile.421) | copy-start | bytes 9220
  355.7 139.8 %copy-start.184 = (f32[768]{0:T(1024)}, f32[768]{0:T(1024)S(1)}, u32[]{:S(2)}) copy-start(f32[768]{0:T(1024)S(1)} %tile.419) | copy-start | bytes 9220
  357.7 137.8 %copy-start.186 = (f32[768]{0:T(1024)}, f32[768]{0:T(1024)S(1)}, u32[]{:S(2)}) copy-start(f32[768]{0:T(1024)S(1)} %tile.417) | copy-start | bytes 9220
  507.5 120.4 %copy-start.208 = (f32[96]{0:T(128)}, f32[96]{0:T(128)S(1)}, u32[]{:S(2)}) copy-start(f32[96]{0:T(128)S(1)} %get-tuple-element.326) | copy-start | bytes 1156
  650.7 82.2 %all-gather.5.cloned.1.call-start = ((), (), s32[]{:S(2)}) async-start(), calls=%async_computation.4 | async-start | bytes 6144000 | tf_op jit(solution)/shard_map/all_gather | solution.py:211
  653.4 182.7 %reduce-scatter.5.cloned.1.call-start = ((), (), s32[]{:S(2)}) async-start(), calls=%async_computation.5 | async-start | bytes 12288000 | tf_op jit(solution)/shard_map/reduce_scatter | solution.py:219
  754.9 133.4 %reduce-scatter.3.cloned.1.call-start = ((), (), s32[]{:S(2)}) async-start(), calls=%async_computation.3 | async-start | bytes 6144000 | tf_op jit(solution)/shard_map/reduce_scatter | solution.py:205
  765.3 1052.4 %all-reduce.193.cloned.1.call-start = ((), (), s32[]{:S(2)}) async-start(), calls=%async_computation.8 | async-start | bytes 237568 | tf_op jit(solution)/shard_map/psum | solution.py:265
  1543.7 137.0 %copy-start.25 = (f32[1,1,8,10,10,768]{5,0,4,3,2,1:T(1,128)}, f32[1,1,8,10,10,768]{5,0,4,3,2,1:T(1,128)S(1)}, u32[]{:S(2)}) copy-start(f32[1,1,8,10,10,768]{5,0,4,3,2,1:T(1,128)S(1)} %fusion.37) | copy-start | bytes 7372804
  1543.7 62.1 %copy-start.36 = (f32[1,8,10,10,768]{4,0,3,2,1:T(1,128)S(1)}, f32[1,8,10,10,768]{4,0,3,2,1:T(1,128)}, u32[]{:S(2)}) copy-start(f32[1,8,10,10,768]{4,0,3,2,1:T(1,128)} %get-tuple-element.161) | copy-start | bytes 7372804
  1543.7 62.1 %copy-start.37 = (f32[1,8,10,10,768]{4,0,3,2,1:T(1,128)S(1)}, f32[1,8,10,10,768]{4,0,3,2,1:T(1,128)}, u32[]{:S(2)}) copy-start(f32[1,8,10,10,768]{4,0,3,2,1:T(1,128)} %get-tuple-element.162) | copy-start | bytes 7372804
  1543.7 62.1 %copy-start.39 = (f32[1,8,10,10,768]{4,0,3,2,1:T(1,128)S(1)}, f32[1,8,10,10,768]{4,0,3,2,1:T(1,128)}, u32[]{:S(2)}) copy-start(f32[1,8,10,10,768]{4,0,3,2,1:T(1,128)} %get-tuple-element.204) | copy-start | bytes 7372804
  1543.7 62.1 %copy-start.40 = (f32[1,8,10,10,768]{4,0,3,2,1:T(1,128)S(1)}, f32[1,8,10,10,768]{4,0,3,2,1:T(1,128)}, u32[]{:S(2)}) copy-start(f32[1,8,10,10,768]{4,0,3,2,1:T(1,128)} %get-tuple-element.205) | copy-start | bytes 7372804
  1543.7 62.1 %copy-start.41 = (f32[1,8,10,10,768]{4,0,3,2,1:T(1,128)S(1)}, f32[1,8,10,10,768]{4,0,3,2,1:T(1,128)}, u32[]{:S(2)}) copy-start(f32[1,8,10,10,768]{4,0,3,2,1:T(1,128)} %get-tuple-element.206) | copy-start | bytes 7372804
  1543.7 62.1 %copy-start.42 = (f32[1,8,10,10,768]{4,0,3,2,1:T(1,128)S(1)}, f32[1,8,10,10,768]{4,0,3,2,1:T(1,128)}, u32[]{:S(2)}) copy-start(f32[1,8,10,10,768]{4,0,3,2,1:T(1,128)} %get-tuple-element.207) | copy-start | bytes 7372804
  1612.3 68.3 %copy-start.26 = (f32[1,1,8,10,10,768]{5,0,4,3,2,1:T(1,128)}, f32[1,1,8,10,10,768]{5,0,4,3,2,1:T(1,128)S(1)}, u32[]{:S(2)}) copy-start(f32[1,1,8,10,10,768]{5,0,4,3,2,1:T(1,128)S(1)} %fusion.38) | copy-start | bytes 7372804
  1612.3 61.8 %copy-start.34 = (f32[1,8,10,10,768]{4,0,3,2,1:T(1,128)S(1)}, f32[1,8,10,10,768]{4,0,3,2,1:T(1,128)}, u32[]{:S(2)}) copy-start(f32[1,8,10,10,768]{4,0,3,2,1:T(1,128)} %get-tuple-element.159) | copy-start | bytes 7372804
  1612.3 61.8 %copy-start.35 = (f32[1,8,10,10,768]{4,0,3,2,1:T(1,128)S(1)}, f32[1,8,10,10,768]{4,0,3,2,1:T(1,128)}, u32[]{:S(2)}) copy-start(f32[1,8,10,10,768]{4,0,3,2,1:T(1,128)} %get-tuple-element.160) | copy-start | bytes 7372804
  1612.3 61.8 %copy-start.43 = (f32[1,8,10,10,768]{4,0,3,2,1:T(1,128)S(1)}, f32[1,8,10,10,768]{4,0,3,2,1:T(1,128)}, u32[]{:S(2)}) copy-start(f32[1,8,10,10,768]{4,0,3,2,1:T(1,128)} %get-tuple-element.179) | copy-start | bytes 7372804
  1612.3 61.8 %copy-start.44 = (f32[1,8,10,10,768]{4,0,3,2,1:T(1,128)S(1)}, f32[1,8,10,10,768]{4,0,3,2,1:T(1,128)}, u32[]{:S(2)}) copy-start(f32[1,8,10,10,768]{4,0,3,2,1:T(1,128)} %get-tuple-element.180) | copy-start | bytes 7372804
  1785.8 206.5 %all-reduce.195.cloned.1.call-start = ((), (), s32[]{:S(2)}) async-start(), calls=%async_computation.9 | async-start | bytes 18874368 | tf_op jit(solution)/shard_map/psum | solution.py:265
  1791.3 279.1 %all-reduce.189.cloned.1.call-start = ((), (), s32[]{:S(2)}) async-start(), calls=%async_computation.6 | async-start | bytes 245760 | tf_op jit(solution)/shard_map/psum | solution.py:264
  1817.7 699.0 %all-reduce.191.cloned.1.call-start = ((), (), s32[]{:S(2)}) async-start(), calls=%async_computation.7 | async-start | bytes 28311552 | tf_op jit(solution)/shard_map/psum | solution.py:264
  (276 other events, 4509.1 us)
Sparse Core Ops, SparseCore 0:
  650.8 41.2 all-gather.2
  694.3 38.5 all-gather.4
  755.1 80.9 reduce-scatter.4
  839.1 49.1 reduce-scatter.2
  1785.9 31.7 all-reduce.192
  1821.3 170.9 all-reduce.194
  1997.6 72.6 all-reduce.188
  2076.3 440.3 all-reduce.190
